TPU v7x, 32 devices: a whole 2x2x4 slice. The times are simulated.
32 devices in a mesh: band: 4 (over x, core), inp: 8 (over z, y).
Axes of the slice: x: 2, y: 2, z: 4, core: 2. Of those that a mesh axis runs over, the one named last changes fastest.
Arguments:
- spectra: float32 [1024, 512, 256], P('inp', 'band'), parts along dimension 1, may hold values from -6 to 6
- delays: int32 [1024], replicated, may hold values from 0 to 127
- owner_bounds: int32 [9], replicated, may hold values from 0 to 4608, as said below
Outputs:
- owned: float32 [128, 7680, 256], P('band', 'inp'), parts along dimension 0
There are 4 independent parts, one for each index of `band`. A program takes and returns all parts, laid end to end along the dimension named above; an argument that names none is the same for every part. Nothing has to cross between parts.
Inputs may be any that keep to these rules, and one draw needn't show every extreme that they name: owner_bounds[0] = 0, owner_bounds[8] = 4608, rising; each owner_bounds[k] lies within 192 of k * 576; every owner holds at most 960 rows and some owner exactly 960.
All inputs are finite; a program needn't handle non-finite values.
Results may differ from a plain program's by a relative error of at most 0.000086.
Values sent between devices are 32-bit elements; how exact they have to be, the bound alone decides.
A program may use at most 256 MiB of HBM per device.

v0:
```python
import math
import jax
import jax.numpy as jnp
from jax import lax
from jax.sharding import PartitionSpec as P

CH = 128
AVG = 4
TILE = 128


def cross_product(left_side, right_side):
    return lax.dot_general(
        left_side,
        right_side,
        (((1,), (1,)), ((), ())),
        precision=lax.Precision.HIGHEST,
        preferred_element_type=jnp.float32,
    )


def pack_tile_rows(real_rows, imag_rows, row_tile):
    pieces = []
    for col_tile in range(row_tile + 1):
        pieces.append(
            jnp.concatenate(
                [
                    real_rows[:, col_tile * TILE : (col_tile + 1) * TILE],
                    imag_rows[:, col_tile * TILE : (col_tile + 1) * TILE],
                ],
                axis=1,
            )
        )
    return jnp.concatenate(pieces, axis=0)


def correct(turned, delays, first_chan):
    inputs, local_chans, row_len = turned.shape
    samples = row_len // 2
    channel = first_chan + jnp.arange(local_chans, dtype=jnp.int32)
    phase_steps = delays[:, None] * channel[None, :] % CH
    phase_angle = (phase_steps.astype(jnp.float32) * (2.0 * math.pi / CH))[:, :, None]
    cos_part = jnp.cos(phase_angle)
    sine_part = jnp.sin(phase_angle)
    real_part = turned[:, :, :samples]
    imag_part = turned[:, :, samples:]
    fixed_re = real_part * cos_part + imag_part * sine_part
    fixed_im = imag_part * cos_part - real_part * sine_part
    local_vis = local_chans // AVG
    direct = jnp.concatenate([fixed_re, fixed_im], axis=2).reshape(inputs, local_vis, AVG * row_len)
    swapped = jnp.concatenate([fixed_im, -fixed_re], axis=2).reshape(
        inputs, local_vis, AVG * row_len
    )
    return (direct, swapped)


def per_device(spectra, delays, owner_bounds):
    n_devices = lax.axis_size("inp")
    my_index = lax.axis_index("inp")
    turned = lax.all_to_all(spectra, "inp", split_axis=1, concat_axis=0, tiled=True)
    inputs, local_chans, row_len = turned.shape
    samples = row_len // 2
    norm_scale = 1.0 / (AVG * samples)
    direct, swapped = correct(turned, delays, my_index * local_chans)
    local_vis = local_chans // AVG
    tile_count = inputs // TILE
    packed_list = []
    for vis_index in range(local_vis):
        left_all = direct[:, vis_index]
        swap_all = swapped[:, vis_index]
        pieces = []
        square_re = cross_product(left_all, left_all) * norm_scale
        square_im = cross_product(swap_all, left_all) * norm_scale
        for row_tile in range(tile_count):
            pieces.append(
                pack_tile_rows(
                    square_re[row_tile * TILE : (row_tile + 1) * TILE],
                    square_im[row_tile * TILE : (row_tile + 1) * TILE],
                    row_tile,
                )
            )
        packed_list.append(jnp.concatenate(pieces, axis=0))
    packed = jnp.stack(packed_list, axis=0)
    rows_total = packed.shape[1]
    block_rows = rows_total // n_devices
    margin_rows = block_rows // 3
    slot_rows = block_rows + 2 * margin_rows
    slot_ids = jnp.arange(slot_rows, dtype=jnp.int32)
    counts = owner_bounds[1:] - owner_bounds[:-1]
    is_live = slot_ids[None, :] < counts[:, None]
    row_index = jnp.where(is_live, owner_bounds[:-1, None] + slot_ids[None, :], 0).reshape(-1)
    picked = jnp.take(packed, row_index, axis=1)
    outgoing = jnp.where(is_live.reshape(-1)[None, :, None], picked, jnp.zeros_like(picked))
    result = lax.all_to_all(outgoing, "inp", split_axis=1, concat_axis=0, tiled=True)
    return result


def solution(mesh):
    placed = (P("inp", "band", None), P(), P())
    return jax.shard_map(
        per_device, mesh=mesh, in_specs=placed, out_specs=P("band", "inp", None), check_vma=False
    )
```

profile of v0, /device:TPU:0, one launch (start us, length us, event | category | flops | bytes accessed | tf_op | source)
XLA Modules:
  0.0 1490.5 jit_solution(15595072913385701790)
XLA Ops:
  0.0 17.8 %copy.17 = f32[128,128,256]{2,0,1:T(8,128)} copy(f32[128,128,256]{2,1,0:T(8,128)} %param.3) | data formatting | bytes 33554432 | tf_op args[0]
  17.8 7.8 all-to-all-start
  28.2 360.2 %all-to-all-done = f32[128,128,256]{2,0,1:T(8,128)} async-done(((f32[128,128,256]{2,0,1:T(8,128)}), f32[128,128,256]{2,0,1:T(8,128)}, u32[]{:S(2)}, u32[]{:S(2)}) %all-to-all-start) | async-done | bytes 16777248 | tf_op jit(solution)/shard_map/all_to_all | solution.py:60
  388.4 15.2 %copy.19 = f32[8,128,16,256]{3,2,1,0:T(8,128)S(1)} copy(f32[8,128,16,256]{3,1,2,0:T(8,128)} %bitcast.2) | data formatting | bytes 33554432 | tf_op jit(solution)/shard_map/all_to_all | solution.py:60
  403.7 8.2 fusion.70
  411.9 17.4 %pad_maximum_fusion.2 = (f32[1024,16,256]{2,1,0:T(8,128)}, f32[1024,16,256]{2,1,0:T(8,128)}) fusion(f32[1024,16,128]{2,1,0:T(8,128)S(1)} %get-tuple-element.5, f32[1024,16,128]{2,1,0:T(8,128)} %get-tuple-element.7, f32[1024,16,128]{2,1,0:T(8,128)S(1)} %get-tuple-element.6), kind=kLoop, calls=%fused_computation.4 | loop fusion | flops 8388608 | bytes 58720256 | tf_op jit(solution)/shard_map/concatenate | solution.py:51
  429.3 20.4 %reshape.164 = f32[1024,4,1024]{2,1,0:T(4,128)} reshape(f32[1024,16,256]{2,1,0:T(8,128)} %get-tuple-element.17) | data formatting | bytes 33554432 | tf_op jit(solution)/shard_map/reshape | solution.py:50
  449.7 20.4 %reshape.165 = f32[1024,4,1024]{2,1,0:T(4,128)} reshape(f32[1024,16,256]{2,1,0:T(8,128)} %get-tuple-element.16) | data formatting | bytes 33554432 | tf_op jit(solution)/shard_map/reshape | solution.py:51
  470.0 70.8 %fusion.71 = (f32[1024,1,1024]{2,1,0:T(1,128)}, f32[1024,1,1024]{2,1,0:T(1,128)S(1)}, f32[1024,1,1024]{2,1,0:T(1,128)}, f32[1024,1,1024]{2,1,0:T(1,128)}, f32[10...) fusion(f32[1024,4,1024]{2,1,0:T(4,128)} %reshape.165, ...), kind=kLoop, calls=%fused_computation.212 | loop fusion | bytes 67108864 | tf_op jit(solution)/shard_map/slice | solution.py:70
  540.8 19.0 %fusion.32 = f32[1024,1024]{0,1:T(8,128)S(1)} fusion(f32[1024,1,1024]{2,1,0:T(1,128)} %get-tuple-element.315), kind=kOutput, calls=%fused_computation.39 | convolution fusion | flops 12885950464 | bytes 8388608 | tf_op jit(solution)/shard_map/dot_general | solution.py:13
  559.9 14.3 fusion.44
  577.2 14.3 fusion.35
  591.5 14.7 fusion.49
  608.7 14.3 fusion.38
  623.0 14.5 fusion.54
  639.3 14.7 fusion.41
  654.0 14.4 fusion.59
  673.7 6.9 pad_maximum_fusion
  680.7 21.5 %copy.22 = f32[4,4608,256]{2,0,1:T(4,128)} copy(f32[4,4608,256]{1,2,0:T(8,128)} %pad_maximum_fusion) | data formatting | bytes 37748736 | tf_op jit(solution)/shard_map/stack | solution.py:83
  702.2 36.3 %gather_fusion = f32[7680,4,256]{2,1,0:T(4,128)} fusion(f32[4,4608,256]{2,0,1:T(4,128)} %copy.22, s32[8192]{0:T(1024)S(1)} %copy-done.50), kind=kCustom, calls=%fused_computation | custom fusion | bytes 62945280 | tf_op jit(solution)/shard_map/jit(_take)/gather | solution.py:92
  738.5 40.9 %select_bitcast_fusion = f32[4,7680,256]{2,0,1:T(4,128)S(1)} fusion(f32[7680,4,256]{2,1,0:T(4,128)} %gather_fusion, pred[7680]{0:T(1024)(128)(4,1)S(1)} %copy-done.52, pred[7680]{0:T(1024)(128)(4,1)S(1)} %copy-done.53), kind=kLoop, calls=%fused_computation.1 | loop fusion | flops 15728640 | bytes 62929920 | tf_op jit(solution)/shard_map/jit(_where)/select_n | solution.py:93
  779.4 683.8 %all_to_all.36 = f32[4,7680,256]{2,0,1:T(4,128)} all-to-all(f32[4,7680,256]{2,0,1:T(4,128)S(1)} %select_bitcast_fusion), channel_id=1, replica_groups=mesh['band'=4,'inp'=8] {'inp'}, dimensions={1} | all-to-all | bytes 62914560 | tf_op jit(solution)/shard_map/all_to_all | solution.py:94
  1463.1 16.4 %copy.23 = f32[4,7680,256]{2,1,0:T(8,128)S(1)} copy(f32[4,7680,256]{2,0,1:T(4,128)} %all_to_all.36) | data formatting | bytes 62914560 | tf_op jit(solution)/shard_map/all_to_all | solution.py:94
  1479.6 10.7 copy.24
  (285 shorter events, 13.1 us)
Async XLA Ops:
  17.8 7.8 copy-start.54
  17.8 8.6 copy-start.55
  17.8 370.6 %all-to-all-start = ((f32[128,128,256]{2,0,1:T(8,128)}), f32[128,128,256]{2,0,1:T(8,128)}, u32[]{:S(2)}, u32[]{:S(2)}) async-start(f32[128,128,256]{2,0,1:T(8,128)} %copy.17), calls=%async_computation | async-start | bytes 33554432 | tf_op jit(solution)/shard_map/all_to_all | solution.py:60
  26.9 376.8 %copy-start.51 = (pred[7680]{0:T(1024)(128)(4,1)}, pred[7680]{0:T(1024)(128)(4,1)S(1)}, u32[]{:S(2)}) copy-start(pred[7680]{0:T(1024)(128)(4,1)S(1)} %lt.59) | copy-start | bytes 23044
  540.8 19.1 %copy-start.4 = (f32[1024,1,1024]{2,1,0:T(1,128)S(1)}, f32[1024,1,1024]{2,1,0:T(1,128)}, u32[]{:S(2)}) copy-start(f32[1024,1,1024]{2,1,0:T(1,128)} %get-tuple-element.8) | copy-start | bytes 12582916
  540.8 19.1 %copy-start.5 = (f32[1024,1,1024]{2,1,0:T(1,128)S(1)}, f32[1024,1,1024]{2,1,0:T(1,128)}, u32[]{:S(2)}) copy-start(f32[1024,1,1024]{2,1,0:T(1,128)} %get-tuple-element.315) | copy-start | bytes 12582916
  574.2 3.1 copy-start.3
  577.2 14.3 copy-start.2
  606.2 2.3 copy-start.1
  608.7 14.3 copy-start
  668.7 2.2 copy-start.18
  668.7 2.2 copy-start.39
  668.7 2.2 copy-start.15
  668.8 2.2 copy-start.38
  668.8 2.2 copy-start.12
  668.8 2.2 copy-start.37
  669.0 2.2 copy-start.27
  669.0 2.2 copy-start.25
  669.0 2.2 copy-start.23
  669.2 2.2 copy-start.11
  669.2 2.2 copy-start.8
  680.6 21.5 %copy-start.50 = (s32[8192]{0:T(1024)S(1)}, s32[8192]{0:T(1024)}, u32[]{:S(2)}) copy-start(s32[8192]{0:T(1024)} %pad_clamp_fusion) | copy-start | bytes 98308
  702.2 36.3 %copy-start.52 = (pred[7680]{0:T(1024)(128)(4,1)S(1)}, pred[7680]{0:T(1024)(128)(4,1)}, u32[]{:S(2)}) copy-start(pred[7680]{0:T(1024)(128)(4,1)} %copy-done.51) | copy-start | bytes 23044
  702.2 36.3 %copy-start.53 = (pred[7680]{0:T(1024)(128)(4,1)S(1)}, pred[7680]{0:T(1024)(128)(4,1)}, u32[]{:S(2)}) copy-start(pred[7680]{0:T(1024)(128)(4,1)} %compare_and_fusion) | copy-start | bytes 23044
  (33 other events, 59.7 us)
where the time goes:
time: 1500 us; the launch traced here: 1490 us
  blocking collectives  684 us (46%)
  waiting for transfers between devices  360 us (24%)
  local copies, waits for them, and re-layouts  238 us (16%)
  matrix products  120 us (8%)
  other arithmetic  78.1 us (5%)
    all_to_all x1, blocking collectives, per_device(): lax.all_to_all(outgoing, 'inp', split_axis=1, concat_axis=0, tiled=True)  684 us
    all_to_all x1, waiting for transfers between devices, per_device(): lax.all_to_all(spectra, 'inp', split_axis=1, concat_axis=0, tiled=True)  360 us
    dot_general x8, matrix products, cross_product(): lax.dot_general(left_side, right_side, (((1,), (1,)), ((), ())), precisio...  120 us
    slice x1, local copies, waits for them, and re-layouts, per_device(): swap_all = swapped[:, vis_index]  70.8 us
    select_n x1, other arithmetic, per_device(): jnp.where(is_live.reshape(-1)[None, :, None], picked, jnp.zeros_like(pick...  40.9 us
    gather x1, local copies, waits for them, and re-layouts, per_device(): picked = jnp.take(packed, row_index, axis=1)  36.3 us
  transfers between devices with their start and end apart: 1, of which 1 were waited for; matrix products, arithmetic and copies ran while one was open for 0% of the time, Pallas kernels for 0%

commit v1 on v0

--- a/solution.py
+++ b/solution.py
@@ -57,7 +57,10 @@
 def per_device(spectra, delays, owner_bounds):
     n_devices = lax.axis_size("inp")
     my_index = lax.axis_index("inp")
-    turned = lax.all_to_all(spectra, "inp", split_axis=1, concat_axis=0, tiled=True)
+    turned = jnp.concatenate(
+        lax.all_to_all(jnp.stack(jnp.split(spectra, lax.axis_size("inp"), axis=1)), "inp", 0, 0),
+        axis=0,
+    )
     inputs, local_chans, row_len = turned.shape
     samples = row_len // 2
     norm_scale = 1.0 / (AVG * samples)

time: 1500 us -> 1490 us (level)
    all_to_all x1 -> x0, local copies, waits for them, and re-layouts: 15.2 us -> none  [per_device(): lax.all_to_all(spectra, 'inp', split_axis=1, concat_axis=0, tiled=True)]
where the time goes in v1:
time: 1490 us; the launch traced here: 1480 us
  blocking collectives  684 us (46%)
  waiting for transfers between devices  360 us (24%)
  local copies, waits for them, and re-layouts  230 us (15%)
  matrix products  120 us (8%)
  other arithmetic  80.1 us (5%)
    all_to_all x1, blocking collectives, per_device(): lax.all_to_all(outgoing, 'inp', split_axis=1, concat_axis=0, tiled=True)  684 us
    all_to_all x1, waiting for transfers between devices, per_device(): lax.all_to_all(jnp.stack(jnp.split(spectra, lax.axis_size('inp'), axis=1)...  360 us
    dot_general x8, matrix products, cross_product(): lax.dot_general(left_side, right_side, (((1,), (1,)), ((), ())), precisio...  120 us
    slice x1, local copies, waits for them, and re-layouts, per_device(): swap_all = swapped[:, vis_index]  70.8 us
    select_n x1, other arithmetic, per_device(): jnp.where(is_live.reshape(-1)[None, :, None], picked, jnp.zeros_like(pick...  40.9 us
    gather x1, local copies, waits for them, and re-layouts, per_device(): picked = jnp.take(packed, row_index, axis=1)  36.3 us
  transfers between devices with their start and end apart: 1, of which 1 were waited for; matrix products, arithmetic and copies ran while one was open for 0% of the time, Pallas kernels for 0%

profile of v1, /device:TPU:0, one launch (start us, length us, event | category | flops | bytes accessed | tf_op | source)
XLA Modules:
  0.0 1483.9 jit_solution(11527213381192768272)
XLA Ops:
  3.1 3.1 bitcast_dynamic-update-slice_fusion.6
  6.2 3.1 bitcast_dynamic-update-slice_fusion.5
  24.8 7.4 all-to-all-start
  34.8 360.3 %all-to-all-done = f32[8,128,16,256]{3,2,1,0:T(8,128)} async-done(((f32[8,128,16,256]{3,2,1,0:T(8,128)}), f32[8,128,16,256]{3,2,1,0:T(8,128)}, u32[]{:S(2)}, u32[]{:S(2)}) %all-to-all-start) | async-done | bytes 16777248 | tf_op jit(solution)/shard_map/all_to_all | solution.py:61
  395.1 10.3 fusion.70
  405.4 17.4 %pad_maximum_fusion.2 = (f32[1024,16,256]{2,1,0:T(8,128)}, f32[1024,16,256]{2,1,0:T(8,128)}) fusion(f32[1024,16,128]{2,1,0:T(8,128)S(1)} %get-tuple-element.5, f32[1024,16,128]{2,1,0:T(8,128)} %get-tuple-element.7, f32[1024,16,128]{2,1,0:T(8,128)S(1)} %get-tuple-element.6), kind=kLoop, calls=%fused_computation.4 | loop fusion | flops 8388608 | bytes 58720256 | tf_op jit(solution)/shard_map/concatenate | solution.py:51
  422.7 20.4 %reshape.168 = f32[1024,4,1024]{2,1,0:T(4,128)} reshape(f32[1024,16,256]{2,1,0:T(8,128)} %get-tuple-element.17) | data formatting | bytes 33554432 | tf_op jit(solution)/shard_map/reshape | solution.py:50
  443.1 20.4 %reshape.169 = f32[1024,4,1024]{2,1,0:T(4,128)} reshape(f32[1024,16,256]{2,1,0:T(8,128)} %get-tuple-element.16) | data formatting | bytes 33554432 | tf_op jit(solution)/shard_map/reshape | solution.py:51
  463.5 70.8 %fusion.71 = (f32[1024,1,1024]{2,1,0:T(1,128)}, f32[1024,1,1024]{2,1,0:T(1,128)S(1)}, f32[1024,1,1024]{2,1,0:T(1,128)}, f32[1024,1,1024]{2,1,0:T(1,128)}, f32[10...) fusion(f32[1024,4,1024]{2,1,0:T(4,128)} %reshape.169, ...), kind=kLoop, calls=%fused_computation.220 | loop fusion | bytes 67108864 | tf_op jit(solution)/shard_map/slice | solution.py:73
  534.3 19.0 %fusion.32 = f32[1024,1024]{0,1:T(8,128)S(1)} fusion(f32[1024,1,1024]{2,1,0:T(1,128)} %get-tuple-element.315), kind=kOutput, calls=%fused_computation.39 | convolution fusion | flops 12885950464 | bytes 8388608 | tf_op jit(solution)/shard_map/dot_general | solution.py:13
  553.3 14.3 fusion.44
  570.6 14.3 fusion.35
  584.9 14.7 fusion.49
  602.1 14.3 fusion.38
  616.4 14.5 fusion.54
  632.7 14.7 fusion.41
  647.4 14.4 fusion.59
  667.1 6.9 pad_maximum_fusion
  674.0 21.5 %copy.12 = f32[4,4608,256]{2,0,1:T(4,128)} copy(f32[4,4608,256]{1,2,0:T(8,128)} %pad_maximum_fusion) | data formatting | bytes 37748736 | tf_op jit(solution)/shard_map/stack | solution.py:86
  695.6 36.3 %gather_fusion = f32[7680,4,256]{2,1,0:T(4,128)} fusion(f32[4,4608,256]{2,0,1:T(4,128)} %copy.12, s32[8192]{0:T(1024)S(1)} %copy-done.50), kind=kCustom, calls=%fused_computation | custom fusion | bytes 62945280 | tf_op jit(solution)/shard_map/jit(_take)/gather | solution.py:95
  731.9 40.9 %select_bitcast_fusion = f32[4,7680,256]{2,0,1:T(4,128)S(1)} fusion(f32[7680,4,256]{2,1,0:T(4,128)} %gather_fusion, pred[7680]{0:T(1024)(128)(4,1)S(1)} %copy-done.52, pred[7680]{0:T(1024)(128)(4,1)S(1)} %copy-done.53), kind=kLoop, calls=%fused_computation.1 | loop fusion | flops 15728640 | bytes 62929920 | tf_op jit(solution)/shard_map/jit(_where)/select_n | solution.py:96
  772.8 683.7 %all_to_all.23 = f32[4,7680,256]{2,0,1:T(4,128)} all-to-all(f32[4,7680,256]{2,0,1:T(4,128)S(1)} %select_bitcast_fusion), channel_id=1, replica_groups=mesh['band'=4,'inp'=8] {'inp'}, dimensions={1} | all-to-all | bytes 62914560 | tf_op jit(solution)/shard_map/all_to_all | solution.py:97
  1456.5 16.4 %copy.13 = f32[4,7680,256]{2,1,0:T(8,128)S(1)} copy(f32[4,7680,256]{2,0,1:T(4,128)} %all_to_all.23) | data formatting | bytes 62914560 | tf_op jit(solution)/shard_map/all_to_all | solution.py:97
  1473.0 10.7 copy.14
  (291 shorter events, 31.7 us)
Async XLA Ops:
  24.8 7.4 copy-start.54
  24.8 8.2 copy-start.55
  24.8 370.3 %all-to-all-start = ((f32[8,128,16,256]{3,2,1,0:T(8,128)}), f32[8,128,16,256]{3,2,1,0:T(8,128)}, u32[]{:S(2)}, u32[]{:S(2)}) async-start(f32[8,128,16,256]{3,2,1,0:T(8,128)} %bitcast_dynamic-update-slice_fusion), calls=%async_computation | async-start | bytes 33554432 | tf_op jit(solution)/shard_map/all_to_all | solution.py:61
  33.5 371.9 %copy-start.51 = (pred[7680]{0:T(1024)(128)(4,1)}, pred[7680]{0:T(1024)(128)(4,1)S(1)}, u32[]{:S(2)}) copy-start(pred[7680]{0:T(1024)(128)(4,1)S(1)} %lt.59) | copy-start | bytes 23044
  534.3 19.0 %copy-start.4 = (f32[1024,1,1024]{2,1,0:T(1,128)S(1)}, f32[1024,1,1024]{2,1,0:T(1,128)}, u32[]{:S(2)}) copy-start(f32[1024,1,1024]{2,1,0:T(1,128)} %get-tuple-element.8) | copy-start | bytes 12582916
  534.3 19.0 %copy-start.5 = (f32[1024,1,1024]{2,1,0:T(1,128)S(1)}, f32[1024,1,1024]{2,1,0:T(1,128)}, u32[]{:S(2)}) copy-start(f32[1024,1,1024]{2,1,0:T(1,128)} %get-tuple-element.315) | copy-start | bytes 12582916
  567.6 3.1 copy-start.3
  570.6 14.3 copy-start.2
  599.6 2.3 copy-start.1
  602.1 14.3 copy-start
  662.1 2.2 copy-start.18
  662.1 2.2 copy-start.39
  662.1 2.2 copy-start.15
  662.1 2.2 copy-start.38
  662.2 2.2 copy-start.12
  662.2 2.2 copy-start.37
  662.4 2.2 copy-start.27
  662.4 2.2 copy-start.25
  662.4 2.2 copy-start.23
  662.6 2.2 copy-start.11
  662.6 2.2 copy-start.8
  674.0 21.5 %copy-start.50 = (s32[8192]{0:T(1024)S(1)}, s32[8192]{0:T(1024)}, u32[]{:S(2)}) copy-start(s32[8192]{0:T(1024)} %pad_clamp_fusion) | copy-start | bytes 98308
  695.6 36.3 %copy-start.52 = (pred[7680]{0:T(1024)(128)(4,1)S(1)}, pred[7680]{0:T(1024)(128)(4,1)}, u32[]{:S(2)}) copy-start(pred[7680]{0:T(1024)(128)(4,1)} %copy-done.51) | copy-start | bytes 23044
  695.6 36.3 %copy-start.53 = (pred[7680]{0:T(1024)(128)(4,1)S(1)}, pred[7680]{0:T(1024)(128)(4,1)}, u32[]{:S(2)}) copy-start(pred[7680]{0:T(1024)(128)(4,1)} %compare_and_fusion) | copy-start | bytes 23044
  (33 other events, 59.7 us)
